TPU v7x, 32 devices: a whole 2x2x4 slice. The times are simulated.
32 devices in a mesh: twin: 2 (over y), gx: 4 (over z), gy: 2 (over core), gz: 2 (over x).
Axes of the slice: x: 2, y: 2, z: 4, core: 2. Of those that a mesh axis runs over, the one named last changes fastest.
Arguments:
- potential: float32 [64, 32, 256], P(('twin', 'gx'), 'gy', 'gz'), parts along dimension 0, may hold values from 0 to 1
- gating: float32 [64, 32, 256], P(('twin', 'gx'), 'gy', 'gz'), parts along dimension 0, may hold values from 0 to 1
- adjoint_v: float32 [64, 32, 256], P(('twin', 'gx'), 'gy', 'gz'), parts along dimension 0, may hold values from -6 to 6
- adjoint_h: float32 [64, 32, 256], P(('twin', 'gx'), 'gy', 'gz'), parts along dimension 0, may hold values from -6 to 6
- recorded: float32 [64, 32, 256], P(('twin', 'gx'), 'gy', 'gz'), parts along dimension 0, may hold values from 0 to 1
- tissue_mask: int32 [64, 32, 256], P(('twin', 'gx'), 'gy', 'gz'), parts along dimension 0, may hold values from 0 to 1
- fibre_sector: int32 [64, 32, 256], P(('twin', 'gx'), 'gy', 'gz'), parts along dimension 0, may hold values from 0 to 11
- region_label: int32 [64, 32, 256], P(('twin', 'gx'), 'gy', 'gz'), parts along dimension 0, may hold values from 0 to 15
- fibre_table: float32 [24, 9], P('twin'), parts along dimension 0, may hold values from 0.005 to 0.025
- conductance: float32 [32], P('twin'), parts along dimension 0, may hold values from 0.5 to 2
Outputs:
- lambda_v: float32 [64, 32, 256], P(('twin', 'gx'), 'gy', 'gz'), parts along dimension 0
- lambda_h: float32 [64, 32, 256], P(('twin', 'gx'), 'gy', 'gz'), parts along dimension 0
- sensitivity: float32 [32], P('twin'), parts along dimension 0
There are 2 independent parts, one for each index of `twin`. A program takes and returns all parts, laid end to end along the dimension named above; each array names one. Nothing has to cross between parts.
All inputs are finite; a program needn't handle non-finite values.
Results may differ from a plain program's by a relative error of at most 0.0003.
Values sent between devices are 32-bit elements; how exact they have to be, the bound alone decides.
A program may use at most 64 MiB of HBM per device.

v0:
```python
import functools
import math

import jax
import jax.numpy as jnp
from jax import lax
from jax.experimental import pallas as pl
from jax.experimental.pallas import tpu as pltpu
from jax.sharding import PartitionSpec as P

WINDOW_STEPS = 3

step_size = 0.1
tau_inward = 0.3
tau_outward = 6.0
tau_opening = 12.0
tau_closing = 15.0
gate_level = 0.13
gate_width = 0.02
gradient_gain = 30.0
PAIR_OFFSETS = (
    (1, 0, 0),
    (0, 1, 0),
    (0, 0, 1),
    (1, 1, 0),
    (1, -1, 0),
    (1, 0, 1),
    (1, 0, -1),
    (0, 1, 1),
    (0, 1, -1),
)
OFFSETS = tuple(
    (d, tuple(sign * part for part in base))
    for d, base in enumerate(PAIR_OFFSETS)
    for sign in (1, -1)
)
VARIANTS = tuple((dy, dz) for dy in (0, 1, -1) for dz in (0, 1, -1))
FLIP = 2
MESH = pl.DeviceIdType.MESH


def moves(size):
    if size == 1:
        return ()
    return (FLIP,) if size == 2 else (1, -1)


def messages(ny, nz):
    found = []
    for mx in (0, 1, -1):
        for my in (0,) + moves(ny):
            for mz in (0,) + moves(nz):
                if 1 <= (mx != 0) + (my != 0) + (mz != 0) <= 2:
                    found.append((mx, my, mz))
    return sorted(found, key=lambda m: (m[0] == 0, m[2] == 0, m[1] == 0))


def land_shape(move, fields, shape):
    lx, ly, lz = shape
    mx, my, mz = move
    if mz:
        return (fields, 8 if my else ly, lz)
    return (fields, 1 if mx else lx, 8 if my else ly, lz)


def kernel(
    counts,
    phase_fields,
    regions,
    sectors,
    scale,
    *refs,
):
    inputs, refs = refs[:10], refs[10:]
    out_v, out_h, out_s = refs[:3]
    held, (load_sem, *refs) = refs[3:13], refs[13:]
    loads = [
        pltpu.make_async_copy(src, dst, load_sem.at[k])
        for k, (src, dst) in enumerate(zip(inputs, held))
    ]
    for load in loads:
        load.start()
    (region_ref, tissue_ref, cond_ref, sector_ref, v_ref, table_ref, h_ref, av_ref, ah_ref, rec_ref) = held
    (coef, grad, diag, vvar, mvar, gathered, red_send, red_recv, *rest) = refs
    nx, ny, nz = counts
    shape = v_ref.shape
    lx, ly, lz = shape
    moved = messages(ny, nz)
    phases = []
    for _ in phase_fields:
        stage = [rest.pop(0) for _ in range(4)]
        land = {move: rest.pop(0) for move in moved}
        phases.append((stage, land, rest.pop(0), rest.pop(0)))

    ix, iy, iz = lax.axis_index("gx"), lax.axis_index("gy"), lax.axis_index("gz")
    n = nx * ny * nz
    me = (ix * ny + iy) * nz + iz

    def device(index):
        return {"gx": index // (ny * nz), "gy": (index // nz) % ny, "gz": index % nz}

    barrier = pltpu.get_barrier_semaphore()

    def greet(rel, carry):
        pl.semaphore_signal(
            barrier, inc=1, device_id=device((me + rel) % n), device_id_type=MESH
        )
        return carry

    def each_other(body):
        if n <= 64:
            for rel in range(1, n):
                body(rel, 0)
        else:
            lax.fori_loop(1, n, body, 0)

    each_other(greet)

    def along(index, count, move):
        if move == 0:
            return index, None
        if move == FLIP:
            return 1 - index, None
        return index + move, (index < count - 1) if move == 1 else (index > 0)

    def both(conds):
        conds = [c for c in conds if c is not None]
        if not conds:
            return None
        out = conds[0]
        for c in conds[1:]:
            out = jnp.logical_and(out, c)
        return out

    def guarded(cond, body):
        if cond is None:
            body()
        else:
            pl.when(cond)(body)

    def copy_of(phase, k):
        (sx, sy, sz, syz), land, send, recv = phases[phase]
        mx, my, mz = move = moved[k]
        tx, cx = along(ix, nx, mx)
        ty, cy = along(iy, ny, my)
        tz, cz = along(iz, nz, mz)
        back = [along(i, c, m if m == FLIP else -m)[1] for i, c, m in
                ((ix, nx, mx), (iy, ny, my), (iz, nz, mz))]
        if mz:
            src = syz if my else sz
        elif my:
            src = sy
            if mx:
                src = sy.at[:, pl.ds(lx - 1 if mx == 1 else 0, 1)]
        else:
            src = sx.at[:, pl.ds(1 if mx == 1 else 0, 1)]
        copy = pltpu.make_async_remote_copy(
            src_ref=src,
            dst_ref=land[move],
            send_sem=send.at[k],
            recv_sem=recv.at[k],
            device_id={"gx": tx, "gy": ty, "gz": tz},
            device_id_type=MESH,
        )
        return copy, both((cx, cy, cz)), both(back)

    lane3 = lax.broadcasted_iota(jnp.int32, (1, 1, lz), 2)
    sub8 = lax.broadcasted_iota(jnp.int32, (8, lz), 0)
    lane = lax.broadcasted_iota(jnp.int32, (ly, lz), 1)
    lane8 = lax.broadcasted_iota(jnp.int32, (8, lz), 1)

    def roll(x, shift, axis):
        size = x.shape[axis]
        shift = shift % size
        return x if shift == 0 else pltpu.roll(x, shift, axis)

    def stage_fields(phase, fields):
        sx, sy, sz, syz = phases[phase][0]
        for f, u in enumerate(fields):
            sx[f, 0] = u[0]
            sx[f, 1] = u[lx - 1]
            sy[f] = jnp.where((sub8 < 4)[None], u[:, :8], u[:, ly - 8 :])
            packed = jnp.zeros((ly, lz), jnp.float32)
            for p in range(lx):
                edge = jnp.where(lane == 0, roll(u[p], 1, 1), roll(u[p], -1, 1))
                here = (lane == 2 * p) | (lane == 2 * p + 1)
                packed = jnp.where(here, roll(edge, 2 * p + 1, 1), packed)
            sz[f] = packed
            syz[f] = jnp.where(sub8 < 4, packed[:8], packed[ly - 8 :])

    def send(phase):
        for k in range(len(moved)):
            copy, cond, _ = copy_of(phase, k)
            guarded(cond, copy.start)

    def receive(phase):
        for k in range(len(moved)):
            copy, _, cond = copy_of(phase, k)
            guarded(cond, copy.wait_recv)

    def finish_sends(phase):
        for k in range(len(moved)):
            copy, cond, _ = copy_of(phase, k)
            guarded(cond, copy.wait_send)

    one = lambda cond: jnp.where(cond, 1, 0)
    has_x = {1: one(ix > 0), -1: one(ix < nx - 1)}
    yp, ym, zp, zm = one(iy < ny - 1), one(iy > 0), one(iz < nz - 1), one(iz > 0)

    def fetch(phase, f, mx, in_y, in_z):
        land = phases[phase][1]
        rows, lanes = (sub8, lane8) if in_y else (None, lane)
        if in_y:
            y_parts = [
                (m, jnp.where(sub8 < 4, yp if m != 1 else 0, ym if m != -1 else 0))
                for m in moves(ny)
            ]
        else:
            y_parts = [(0, None)]
        if in_z:
            z_parts = [
                (m, jnp.where(lanes % 2 == 0, zp if m != 1 else 0, zm if m != -1 else 0))
                for m in moves(nz)
            ]
        else:
            z_parts = [(0, None)]
        out = None
        for my, cy in y_parts:
            for mz, cz in z_parts:
                value = land[(mx, my, mz)][f]
                ok = has_x[mx] if mx else 1
                for c in (cy, cz):
                    if c is not None:
                        ok = c * ok
                keep = jnp.broadcast_to(ok, value.shape[-2:]) > 0
                if value.ndim == 3:
                    keep = keep[None]
                other = jnp.zeros_like(value) if out is None else out
                out = jnp.where(jnp.broadcast_to(keep, value.shape), value, other)
        return out

    def halo(phase, f):
        return dict(
            x={m: fetch(phase, f, m, False, False)[0] for m in (1, -1)},
            y=fetch(phase, f, 0, True, False),
            xy={m: fetch(phase, f, m, True, False)[0] for m in (1, -1)},
            z=fetch(phase, f, 0, False, True),
            xz={m: fetch(phase, f, m, False, True) for m in (1, -1)},
            yz=fetch(phase, f, 0, True, True),
        )

    def extend(u, parts):
        middle = jnp.concatenate([u, parts["y"]], axis=1)
        ends = {m: jnp.concatenate([parts["x"][m], parts["xy"][m]], axis=0) for m in (1, -1)}
        planes = [ends[1]] + [middle[p] for p in range(lx)] + [ends[-1]]
        z_rows = jnp.concatenate([parts["z"], parts["yz"]], axis=0)
        edges = (
            [roll(parts["xz"][1], -(2 * lx - 1), 1)]
            + [roll(z_rows, -(2 * p + 1), 1) for p in range(lx)]
            + [roll(parts["xz"][-1], -1, 1)]
        )
        return planes, edges

    def variant(ext, dy, dz, p):
        planes, edges = ext
        x = planes[p]
        outer = p in (0, lx + 1)
        if outer and dy and dz:
            return None
        if dz:
            rows = ly if dy == 0 else ly + 8
            at = lax.broadcasted_iota(jnp.int32, (rows, lz), 1)
            x = jnp.where(
                at == (lz - 1 if dz == 1 else 0), edges[p][:rows], roll(x[:rows], -dz, 1)
            )
        if dy:
            x = roll(x, -dy, 0)
        return x[:ly]

    def store_variants(ref, where, ext):
        for k, (dy, dz) in enumerate(VARIANTS):
            for p in range(lx + 2):
                x = variant(ext, dy, dz, p)
                if x is not None:
                    ref[where, k, p] = x

    def neighbour(ref, where, offset, p):
        return ref[where, VARIANTS.index(offset[1:]), p + 1 + offset[0]]

    for load in loads[:5]:
        load.wait()
    tissue = tissue_ref[...].astype(jnp.float32)
    factor = jnp.zeros(shape, jnp.float32)
    for label in range(regions):
        factor = jnp.where(region_ref[...] == label, cond_ref[label], factor)
    factor = tissue * factor
    sector = sector_ref[...].astype(jnp.float32)
    stage_fields(0, (factor, sector, v_ref[...]))
    pl.semaphore_wait(barrier, n - 1)
    send(0)
    for load in loads[5:]:
        load.wait()

    def fibres(codes):
        found = [jnp.zeros(codes.shape, jnp.float32) for _ in PAIR_OFFSETS]
        for label in range(sectors):
            same = codes == float(label)
            for d in range(len(PAIR_OFFSETS)):
                found[d] = jnp.where(same, table_ref[label, d], found[d])
        return found

    def ionic(volts, gate):
        s = 1.0 / (1.0 + jnp.exp(-(volts - gate_level) / gate_width))
        drive_v = gate * volts * volts * (1.0 - volts) / tau_inward - volts / tau_outward
        drive_h = (1.0 - s) * (1.0 - gate) / tau_opening - s * gate / tau_closing
        return drive_v, drive_h

    def partials(volts, gate):
        s = 1.0 / (1.0 + jnp.exp(-(volts - gate_level) / gate_width))
        slope = s * (1.0 - s) / gate_width
        vv = gate * (2.0 * volts - 3.0 * volts * volts) / tau_inward - 1.0 / tau_outward
        vh = volts * volts * (1.0 - volts) / tau_inward
        hv = slope * (-(1.0 - gate) / tau_opening - gate / tau_closing)
        hh = -(1.0 - s) / tau_opening - s / tau_closing
        return vv, vh, hv, hh

    def spread(ref, where, u, p):
        total = -diag[p] * u
        for o, (_, offset) in enumerate(OFFSETS):
            total = total + coef[o, p] * neighbour(ref, where, offset, p)
        return total

    fibre = fibres(sector)
    flux = [factor * f for f in fibre]
    volts, gate = v_ref[...], h_ref[...]
    drive_v, drive_h = ionic(volts, gate)

    receive(0)
    fac_halo = halo(0, 0)
    sec_halo = halo(0, 1)
    fac_ext = extend(factor, fac_halo)

    halo_flux = [dict() for _ in PAIR_OFFSETS]
    for name in fac_halo:
        entry, codes = fac_halo[name], sec_halo[name]
        if isinstance(entry, dict):
            for d in range(len(PAIR_OFFSETS)):
                halo_flux[d][name] = {}
            for m in entry:
                for d, f in enumerate(fibres(codes[m])):
                    halo_flux[d][name][m] = entry[m] * f
        else:
            for d, f in enumerate(fibres(codes)):
                halo_flux[d][name] = entry * f

    beside = {}
    for dy, dz in VARIANTS:
        beside[dy, dz] = [
            None if x is None else jnp.where(x > 0.0, 1.0, 0.0)
            for x in (variant(fac_ext, dy, dz, p) for p in range(lx + 2))
        ]
    for o, (d, offset) in enumerate(OFFSETS):
        dx, dy, dz = offset
        ext = extend(flux[d], halo_flux[d])
        for p in range(lx):
            near = beside[dy, dz][p + 1 + dx]
            c = 0.5 * (flux[d][p] * near + variant(ext, dy, dz, p + 1 + dx) * tissue[p])
            coef[o, p] = c
            diag[p] = c if o == 0 else diag[p] + c
            grad[o, p] = (-0.5 * tissue[p]) * near * fibre[d][p]

    volts_at, gate_at = [], []
    for step in range(WINDOW_STEPS):
        volts_at.append(volts)
        gate_at.append(gate)
        if step:
            stage_fields(step, (volts,))
            send(step)
            drive_v, drive_h = ionic(volts, gate)
        base = volts + tissue * (step_size * drive_v)
        gate = gate + tissue * (step_size * drive_h)
        if step:
            receive(step)
        store_variants(vvar, step, extend(volts, halo(step, 0 if step else 2)))
        volts = jnp.stack(
            [base[p] + tissue[p] * spread(vvar, step, volts[p], p) for p in range(lx)]
        )

    back_v = av_ref[...] + tissue * (volts - rec_ref[...])
    back_h = ah_ref[...]
    terms = jnp.zeros(shape, jnp.float32)

    def add_terms(terms, step, masked):
        rows = []
        for p in range(lx):
            total = terms[p]
            mid_m, mid_v = masked[p], volts_at[step][p]
            for o, (_, offset) in enumerate(OFFSETS):
                total = total + grad[o, p] * (
                    (neighbour(mvar, step, offset, p) - mid_m)
                    * (neighbour(vvar, step, offset, p) - mid_v)
                )
            rows.append(total)
        return jnp.stack(rows)

    pending = None
    phase = WINDOW_STEPS
    for step in reversed(range(WINDOW_STEPS)):
        masked = tissue * back_v
        stage_fields(phase, (masked,))
        send(phase)
        if pending is not None:
            terms = add_terms(terms, *pending)
        vv, vh, hv, hh = partials(volts_at[step], gate_at[step])
        base = back_v + step_size * tissue * (vv * back_v + hv * back_h)
        back_h = back_h + step_size * tissue * (vh * back_v + hh * back_h)
        receive(phase)
        store_variants(mvar, step, extend(masked, halo(phase, 0)))
        if step:
            back_v = jnp.stack(
                [base[p] + spread(mvar, step, masked[p], p) for p in range(lx)]
            )
        pending = (step, masked)
        phase += 1

    terms = add_terms(terms, *pending)
    row = lax.broadcasted_iota(jnp.int32, (8, lz), 0)
    column = lax.broadcasted_iota(jnp.int32, (1, lz), 1)
    sums = jnp.zeros((1, lz), jnp.float32)
    region = region_ref[...]
    for label in range(regions):
        own = jnp.sum(jnp.where(region == label, terms, 0.0), axis=(0, 1))[None]
        own = jnp.sum(own, axis=1, keepdims=True)
        sums = jnp.where(column == label, own, sums)
    gathered[me] = jnp.where(row == 0, jnp.broadcast_to(sums, (8, lz)), 0.0)

    def red_copy(slot, rel):
        return pltpu.make_async_remote_copy(
            src_ref=gathered.at[me],
            dst_ref=gathered.at[slot],
            send_sem=red_send.at[rel],
            recv_sem=red_recv.at[slot],
            device_id=device((me + rel) % n),
            device_id_type=MESH,
        )

    def red_start(rel, carry):
        red_copy(me, rel).start()
        return carry

    def red_wait(rel, carry):
        red_copy((me + rel) % n, rel).wait_recv()
        return carry

    def red_finish(rel, carry):
        red_copy(me, rel).wait_send()
        return carry

    each_other(red_start)
    for p in range(lx):
        out_v[p] = base[p] + spread(mvar, 0, masked[p], p)
    out_h[...] = back_h
    for k in range(len(phase_fields)):
        finish_sends(k)
    each_other(red_wait)
    total = jnp.sum(gathered[...], axis=0)[0:1] * scale
    out_s[...] = total[0, :regions]
    each_other(red_finish)


def local(*args):
    potential, fibre_table, conductance = args[0], args[8], args[9]
    counts = tuple(lax.axis_size(a) for a in ("gx", "gy", "gz"))
    nx, ny, nz = counts
    shape = potential.shape
    lx, ly, lz = shape
    regions, sectors = conductance.shape[0], fibre_table.shape[0]
    cells = lx * ly * lz * nx * ny * nz
    scale = gradient_gain / math.sqrt(cells / regions)
    phase_fields = (3,) + (1,) * (2 * WINDOW_STEPS - 1)
    f32 = jnp.float32
    pairs = len(OFFSETS)
    variants = len(VARIANTS)
    n = nx * ny * nz
    order = (7, 5, 9, 6, 0, 8, 1, 2, 3, 4)
    operands = [args[k] for k in order]
    scratch = [
        (pltpu.SMEM if k >= 8 else pltpu.VMEM)(args[k].shape, args[k].dtype) for k in order
    ]
    scratch += [
        pltpu.SemaphoreType.DMA((len(order),)),
        pltpu.VMEM((pairs,) + shape, f32),
        pltpu.VMEM((pairs,) + shape, f32),
        pltpu.VMEM(shape, f32),
        pltpu.VMEM((WINDOW_STEPS, variants, lx + 2, ly, lz), f32),
        pltpu.VMEM((WINDOW_STEPS, variants, lx + 2, ly, lz), f32),
        pltpu.VMEM((n, 8, lz), f32),
        pltpu.SemaphoreType.DMA((n,)),
        pltpu.SemaphoreType.DMA((n,)),
    ]
    moved = messages(ny, nz)
    for fields in phase_fields:
        scratch += [
            pltpu.VMEM((fields, 2, ly, lz), f32),
            pltpu.VMEM((fields, lx, 8, lz), f32),
            pltpu.VMEM((fields, ly, lz), f32),
            pltpu.VMEM((fields, 8, lz), f32),
        ]
        scratch += [pltpu.VMEM(land_shape(move, fields, shape), f32) for move in moved]
        scratch += [pltpu.SemaphoreType.DMA((len(moved),))] * 2
    vmem = pl.BlockSpec(memory_space=pltpu.VMEM)
    hbm = pl.BlockSpec(memory_space=pltpu.HBM)
    return pl.pallas_call(
        functools.partial(kernel, counts, phase_fields, regions, sectors, scale),
        out_shape=(
            jax.ShapeDtypeStruct(shape, f32),
            jax.ShapeDtypeStruct(shape, f32),
            jax.ShapeDtypeStruct((regions,), f32),
        ),
        in_specs=[hbm] * len(order),
        out_specs=(vmem, vmem, vmem),
        scratch_shapes=scratch,
        compiler_params=pltpu.CompilerParams(
            collective_id=0, has_side_effects=True, vmem_limit_bytes=40 * 2**20
        ),
        name="adjoint_window",
    )(*operands)


def solution(mesh):
    block = P(("twin", "gx"), "gy", "gz")
    in_specs = (block,) * 8 + (P("twin", None), P("twin"))
    out_specs = (block, block, P("twin"))
    return jax.shard_map(local, mesh=mesh, in_specs=in_specs, out_specs=out_specs, check_vma=False)
```

profile of v0, /device:TPU:0, one launch (start us, length us, event | category | flops | bytes accessed | tf_op | source)
XLA Modules:
  0.0 44.5 jit_solution(8890630196522114508)
XLA Ops:
  0.6 0.0 copy-start
  0.6 0.8 %copy-done = s32[8,16,128]{2,1,0:T(8,128)S(1)} copy-done((s32[8,16,128]{2,1,0:T(8,128)S(1)}, s32[8,16,128]{2,1,0:T(8,128)}, u32[]{:S(2)}) %copy-start) | copy-done | bytes 65560
  1.5 0.0 copy-start.1
  1.5 0.8 %copy-done.1 = s32[8,16,128]{2,1,0:T(8,128)S(1)} copy-done((s32[8,16,128]{2,1,0:T(8,128)S(1)}, s32[8,16,128]{2,1,0:T(8,128)}, u32[]{:S(2)}) %copy-start.1) | copy-done | bytes 65560
  2.3 0.0 copy-start.2
  2.3 0.8 %copy-done.2 = s32[8,16,128]{2,1,0:T(8,128)S(1)} copy-done((s32[8,16,128]{2,1,0:T(8,128)S(1)}, s32[8,16,128]{2,1,0:T(8,128)}, u32[]{:S(2)}) %copy-start.2) | copy-done | bytes 65560
  3.2 0.0 copy-start.3
  3.2 0.8 %copy-done.3 = f32[8,16,128]{2,1,0:T(8,128)S(1)} copy-done((f32[8,16,128]{2,1,0:T(8,128)S(1)}, f32[8,16,128]{2,1,0:T(8,128)}, u32[]{:S(2)}) %copy-start.3) | copy-done | bytes 65560
  4.0 0.0 copy-start.4
  4.0 0.8 %copy-done.4 = f32[8,16,128]{2,1,0:T(8,128)S(1)} copy-done((f32[8,16,128]{2,1,0:T(8,128)S(1)}, f32[8,16,128]{2,1,0:T(8,128)}, u32[]{:S(2)}) %copy-start.4) | copy-done | bytes 65560
  4.8 0.0 copy-start.5
  4.8 0.8 %copy-done.5 = f32[8,16,128]{2,1,0:T(8,128)S(1)} copy-done((f32[8,16,128]{2,1,0:T(8,128)S(1)}, f32[8,16,128]{2,1,0:T(8,128)}, u32[]{:S(2)}) %copy-start.5) | copy-done | bytes 65560
  5.7 0.0 copy-start.6
  5.7 0.8 %copy-done.6 = f32[8,16,128]{2,1,0:T(8,128)S(1)} copy-done((f32[8,16,128]{2,1,0:T(8,128)S(1)}, f32[8,16,128]{2,1,0:T(8,128)}, u32[]{:S(2)}) %copy-start.6) | copy-done | bytes 65560
  6.5 0.0 copy-start.7
  6.5 0.8 %copy-done.7 = f32[8,16,128]{2,1,0:T(8,128)S(1)} copy-done((f32[8,16,128]{2,1,0:T(8,128)S(1)}, f32[8,16,128]{2,1,0:T(8,128)}, u32[]{:S(2)}) %copy-start.7) | copy-done | bytes 65560
  7.4 0.0 copy-start.8
  7.4 0.7 %copy-done.8 = f32[12,9]{1,0:T(8,128)S(1)} copy-done((f32[12,9]{1,0:T(8,128)S(1)}, f32[12,9]{1,0:T(8,128)}, u32[]{:S(2)}) %copy-start.8) | copy-done | bytes 456
  8.1 0.0 copy-start.9
  8.1 0.7 %copy-done.9 = f32[16]{0:T(128)S(1)} copy-done((f32[16]{0:T(128)S(1)}, f32[16]{0:T(128)}, u32[]{:S(2)}) %copy-start.9) | copy-done | bytes 88
  8.7 34.0 %adjoint_window.1 = (f32[8,16,128]{2,1,0:T(8,128)S(1)}, f32[8,16,128]{2,1,0:T(8,128)S(1)}, f32[16]{0:T(128)S(1)}) custom-call(s32[8,16,128]{2,1,0:T(8,128)S(1)} %copy-done, s32[8,16,128]{2,1,0:T(8,128)S(1)} %copy-done.1, f32[16]{0:T(128)S(1)} %copy-done.9, s32[8,16,128]{2,1,0:T(8,128)S(1)} %copy-done.2, f32[8,16,128]{2,1,0:T(8,128)S(1)} %copy-done.3, ...), custom_call_target="tpu_custom_call" | custom-call | tf_op jit(solution)/shard_map/adjoint_window/pallas_call | solution.py:513
  42.8 0.6 %copy.16 = f32[8,16,128]{2,1,0:T(8,128)} copy(f32[8,16,128]{2,1,0:T(8,128)S(1)} %get-tuple-element.6) | data formatting | bytes 131072
  43.4 0.6 %copy.17 = f32[8,16,128]{2,1,0:T(8,128)} copy(f32[8,16,128]{2,1,0:T(8,128)S(1)} %get-tuple-element.7) | data formatting | bytes 131072
  44.0 0.5 %copy.18 = f32[16]{0:T(128)} copy(f32[16]{0:T(128)S(1)} %get-tuple-element.8) | data formatting | bytes 128
Async XLA Ops:
  0.6 0.8 %copy-start = (s32[8,16,128]{2,1,0:T(8,128)S(1)}, s32[8,16,128]{2,1,0:T(8,128)}, u32[]{:S(2)}) copy-start(s32[8,16,128]{2,1,0:T(8,128)} %refs_0_.1) | copy-start | bytes 196612
  1.5 0.8 %copy-start.1 = (s32[8,16,128]{2,1,0:T(8,128)S(1)}, s32[8,16,128]{2,1,0:T(8,128)}, u32[]{:S(2)}) copy-start(s32[8,16,128]{2,1,0:T(8,128)} %refs_1_.1) | copy-start | bytes 196612
  2.3 0.8 %copy-start.2 = (s32[8,16,128]{2,1,0:T(8,128)S(1)}, s32[8,16,128]{2,1,0:T(8,128)}, u32[]{:S(2)}) copy-start(s32[8,16,128]{2,1,0:T(8,128)} %refs_3_.1) | copy-start | bytes 196612
  3.2 0.8 %copy-start.3 = (f32[8,16,128]{2,1,0:T(8,128)S(1)}, f32[8,16,128]{2,1,0:T(8,128)}, u32[]{:S(2)}) copy-start(f32[8,16,128]{2,1,0:T(8,128)} %refs_4_.1) | copy-start | bytes 196612
  4.0 0.8 %copy-start.4 = (f32[8,16,128]{2,1,0:T(8,128)S(1)}, f32[8,16,128]{2,1,0:T(8,128)}, u32[]{:S(2)}) copy-start(f32[8,16,128]{2,1,0:T(8,128)} %refs_6_.1) | copy-start | bytes 196612
  4.8 0.8 %copy-start.5 = (f32[8,16,128]{2,1,0:T(8,128)S(1)}, f32[8,16,128]{2,1,0:T(8,128)}, u32[]{:S(2)}) copy-start(f32[8,16,128]{2,1,0:T(8,128)} %refs_7_.1) | copy-start | bytes 196612
  5.7 0.8 %copy-start.6 = (f32[8,16,128]{2,1,0:T(8,128)S(1)}, f32[8,16,128]{2,1,0:T(8,128)}, u32[]{:S(2)}) copy-start(f32[8,16,128]{2,1,0:T(8,128)} %refs_8_.1) | copy-start | bytes 196612
  6.5 0.8 %copy-start.7 = (f32[8,16,128]{2,1,0:T(8,128)S(1)}, f32[8,16,128]{2,1,0:T(8,128)}, u32[]{:S(2)}) copy-start(f32[8,16,128]{2,1,0:T(8,128)} %refs_9_.1) | copy-start | bytes 196612
  7.4 0.7 %copy-start.8 = (f32[12,9]{1,0:T(8,128)S(1)}, f32[12,9]{1,0:T(8,128)}, u32[]{:S(2)}) copy-start(f32[12,9]{1,0:T(8,128)} %refs_5_.1) | copy-start | bytes 1300
  8.1 0.7 %copy-start.9 = (f32[16]{0:T(128)S(1)}, f32[16]{0:T(128)}, u32[]{:S(2)}) copy-start(f32[16]{0:T(128)} %refs_2_.1) | copy-start | bytes 196
where the time goes:
time: 45.1 us; the launch traced here: 44.5 us
  Pallas kernels  34 us (75%)
  local copies, waits for them, and re-layouts  9.83 us (22%)
  between operations  0.66 us (1%)
    pallas_call x1, Pallas kernels, local(): pl.pallas_call(functools.partial(kernel, counts, phase_fields, regions, s...  34 us
    unnamed x23, local copies, waits for them, and re-layouts  9.83 us

commit v1 on v0

--- a/solution.py
+++ b/solution.py
@@ -521,7 +521,7 @@
         out_specs=(vmem, vmem, vmem),
         scratch_shapes=scratch,
         compiler_params=pltpu.CompilerParams(
-            collective_id=0, has_side_effects=True, vmem_limit_bytes=40 * 2**20
+            collective_id=0, has_side_effects=True, vmem_limit_bytes=63 * 2**20
         ),
         name="adjoint_window",
     )(*operands)

time: 45.1 us -> 37.6 us (0.83)
  local copies, waits for them, and re-layouts: 9.83 us -> 2.65 us
    unnamed x23 -> x7, local copies, waits for them, and re-layouts: 9.83 us -> 2.65 us
where the time goes in v1:
time: 37.6 us; the launch traced here: 37.4 us
  Pallas kernels  34.1 us (91%)
  local copies, waits for them, and re-layouts  2.65 us (7%)
  between operations  0.65 us (2%)
    pallas_call x1, Pallas kernels, local(): pl.pallas_call(functools.partial(kernel, counts, phase_fields, regions, s...  34.1 us
    unnamed x7, local copies, waits for them, and re-layouts  2.65 us

profile of v1, /device:TPU:0, one launch (start us, length us, event | category | flops | bytes accessed | tf_op | source)
XLA Modules:
  0.0 37.4 jit_solution(4585709984824723816)
XLA Ops:
  0.6 34.1 %adjoint_window.1 = (f32[8,16,128]{2,1,0:T(8,128)}, f32[8,16,128]{2,1,0:T(8,128)}, f32[16]{0:T(128)}) custom-call(s32[8,16,128]{2,1,0:T(8,128)} %refs_0_.1, s32[8,16,128]{2,1,0:T(8,128)} %refs_1_.1, f32[16]{0:T(128)} %refs_2_.1, s32[8,16,128]{2,1,0:T(8,128)} %refs_3_.1, f32[8,16,128]{2,1,0:T(8,128)} %refs_4_.1, f32[12,9]{1,0:T(8,128)} %refs_5_.1, ...), custom_call_target="tpu_custom_call" | custom-call | tf_op jit(solution)/shard_map/adjoint_window/pallas_call | solution.py:513
  34.7 0.0 copy-start
  34.7 1.5 %copy.16 = f32[8,16,128]{2,1,0:T(8,128)} copy(f32[8,16,128]{2,1,0:T(8,128)} %get-tuple-element.6) | data formatting | bytes 131072
  36.3 0.0 copy-done
  36.3 0.0 copy-start.1
  36.3 0.6 %copy.17 = f32[8,16,128]{2,1,0:T(8,128)} copy(f32[8,16,128]{2,1,0:T(8,128)S(1)} %copy-done) | data formatting | bytes 131072
  36.9 0.0 copy-done.1
  36.9 0.5 %copy.18 = f32[16]{0:T(128)} copy(f32[16]{0:T(128)S(1)} %copy-done.1) | data formatting | bytes 128
Async XLA Ops:
  34.7 1.5 %copy-start = (f32[8,16,128]{2,1,0:T(8,128)S(1)}, f32[8,16,128]{2,1,0:T(8,128)}, u32[]{:S(2)}) copy-start(f32[8,16,128]{2,1,0:T(8,128)} %get-tuple-element.7) | copy-start | bytes 196612
  36.3 0.6 %copy-start.1 = (f32[16]{0:T(128)S(1)}, f32[16]{0:T(128)}, u32[]{:S(2)}) copy-start(f32[16]{0:T(128)} %get-tuple-element.8) | copy-start | bytes 196

commit v2 on v1

--- a/solution.py
+++ b/solution.py
@@ -81,6 +81,7 @@
     for load in loads:
         load.start()
     (region_ref, tissue_ref, cond_ref, sector_ref, v_ref, table_ref, h_ref, av_ref, ah_ref, rec_ref) = held
+    (final_v, final_h, final_s, save_sem, *refs) = refs
     (coef, grad, diag, vvar, mvar, gathered, red_send, red_recv, *rest) = refs
     nx, ny, nz = counts
     shape = v_ref.shape
@@ -101,18 +102,30 @@
 
     barrier = pltpu.get_barrier_semaphore()
 
-    def greet(rel, carry):
-        pl.semaphore_signal(
-            barrier, inc=1, device_id=device((me + rel) % n), device_id_type=MESH
-        )
-        return carry
+    def wrapped(index, count, by):
+        if by == 0:
+            return index
+        moved_on = index + by
+        return jnp.where(moved_on >= count, moved_on - count, moved_on)
+
+    def greet(rel, slot, target):
+        pl.semaphore_signal(barrier, inc=1, device_id=target, device_id_type=MESH)
 
     def each_other(body):
         if n <= 64:
-            for rel in range(1, n):
-                body(rel, 0)
+            for rel in range(n - 1, 0, -1):
+                tx = wrapped(ix, nx, rel // (ny * nz))
+                ty = wrapped(iy, ny, rel // nz % ny)
+                tz = wrapped(iz, nz, rel % nz)
+                body(rel, (tx * ny + ty) * nz + tz, {"gx": tx, "gy": ty, "gz": tz})
         else:
-            lax.fori_loop(1, n, body, 0)
+
+            def step(rel, carry):
+                slot = (me + rel) % n
+                body(rel, slot, device(slot))
+                return carry
+
+            lax.fori_loop(1, n, step, 0)
 
     each_other(greet)
 
@@ -434,38 +447,57 @@
         sums = jnp.where(column == label, own, sums)
     gathered[me] = jnp.where(row == 0, jnp.broadcast_to(sums, (8, lz)), 0.0)
 
-    def red_copy(slot, rel):
+    def red_copy(rel, slot, target):
         return pltpu.make_async_remote_copy(
             src_ref=gathered.at[me],
             dst_ref=gathered.at[slot],
             send_sem=red_send.at[rel],
             recv_sem=red_recv.at[slot],
-            device_id=device((me + rel) % n),
+            device_id=target,
             device_id_type=MESH,
         )
 
-    def red_start(rel, carry):
-        red_copy(me, rel).start()
-        return carry
-
-    def red_wait(rel, carry):
-        red_copy((me + rel) % n, rel).wait_recv()
-        return carry
-
-    def red_finish(rel, carry):
-        red_copy(me, rel).wait_send()
-        return carry
+    def red_start(rel, slot, target):
+        red_copy(rel, me, target).start()
+
+    def red_wait(rel, slot, target):
+        red_copy(rel, slot, target).wait_recv()
+
+    def red_finish(rel, slot, target):
+        red_copy(rel, me, target).wait_send()
 
     each_other(red_start)
     for p in range(lx):
-        out_v[p] = base[p] + spread(mvar, 0, masked[p], p)
-    out_h[...] = back_h
+        final_v[p] = base[p] + spread(mvar, 0, masked[p], p)
+    final_h[...] = back_h
+    saves = [
+        pltpu.make_async_copy(src, dst, save_sem.at[k])
+        for k, (src, dst) in enumerate(((final_v, out_v), (final_h, out_h), (final_s, out_s)))
+    ]
+    saves[0].start()
+    saves[1].start()
     for k in range(len(phase_fields)):
         finish_sends(k)
     each_other(red_wait)
     total = jnp.sum(gathered[...], axis=0)[0:1] * scale
-    out_s[...] = total[0, :regions]
+    final_s[...] = jnp.broadcast_to(total, (8, lz))
+    saves[2].start()
     each_other(red_finish)
+    for save in saves:
+        save.wait()
+
+
+def hand_out(in_v, in_h, in_s, out_v, out_h, out_s, row, sem):
+    copies = [
+        pltpu.make_async_copy(src, dst, sem.at[k])
+        for k, (src, dst) in enumerate(((in_s, row), (in_v, out_v), (in_h, out_h)))
+    ]
+    for copy in copies:
+        copy.start()
+    copies[0].wait()
+    out_s[...] = row[0, : out_s.shape[0]]
+    for copy in copies[1:]:
+        copy.wait()
 
 
 def local(*args):
@@ -489,6 +521,10 @@
     ]
     scratch += [
         pltpu.SemaphoreType.DMA((len(order),)),
+        pltpu.VMEM(shape, f32),
+        pltpu.VMEM(shape, f32),
+        pltpu.VMEM((8, lz), f32),
+        pltpu.SemaphoreType.DMA((3,)),
         pltpu.VMEM((pairs,) + shape, f32),
         pltpu.VMEM((pairs,) + shape, f32),
         pltpu.VMEM(shape, f32),
@@ -510,21 +546,34 @@
         scratch += [pltpu.SemaphoreType.DMA((len(moved),))] * 2
     vmem = pl.BlockSpec(memory_space=pltpu.VMEM)
     hbm = pl.BlockSpec(memory_space=pltpu.HBM)
-    return pl.pallas_call(
+    back_v, back_h, totals = pl.pallas_call(
         functools.partial(kernel, counts, phase_fields, regions, sectors, scale),
         out_shape=(
             jax.ShapeDtypeStruct(shape, f32),
             jax.ShapeDtypeStruct(shape, f32),
-            jax.ShapeDtypeStruct((regions,), f32),
+            jax.ShapeDtypeStruct((8, lz), f32),
         ),
         in_specs=[hbm] * len(order),
-        out_specs=(vmem, vmem, vmem),
+        out_specs=(hbm, hbm, hbm),
         scratch_shapes=scratch,
         compiler_params=pltpu.CompilerParams(
             collective_id=0, has_side_effects=True, vmem_limit_bytes=63 * 2**20
         ),
         name="adjoint_window",
     )(*operands)
+    return pl.pallas_call(
+        hand_out,
+        out_shape=(
+            jax.ShapeDtypeStruct(shape, f32),
+            jax.ShapeDtypeStruct(shape, f32),
+            jax.ShapeDtypeStruct((regions,), f32),
+        ),
+        in_specs=[hbm] * 3,
+        out_specs=(hbm, hbm, vmem),
+        scratch_shapes=[pltpu.VMEM((8, lz), f32), pltpu.SemaphoreType.DMA((3,))],
+        compiler_params=pltpu.CompilerParams(vmem_limit_bytes=63 * 2**20),
+        name="hand_out",
+    )(back_v, back_h, totals)
 
 
 def solution(mesh):

time: 37.6 us -> 40.9 us (1.088)
  Pallas kernels: 34.1 us -> 40.1 us
  local copies, waits for them, and re-layouts: 2.65 us -> 0 us
    pallas_call x0 -> x1, Pallas kernels: none -> 5.61 us  [local(): pl.pallas_call(hand_out, out_shape=(jax.ShapeDtypeStruct(shape, f32), jax...]
    unnamed x7 -> x0, local copies, waits for them, and re-layouts: 2.65 us -> none
where the time goes in v2:
time: 40.9 us; the launch traced here: 40.7 us
  Pallas kernels  40.1 us (98%)
  between operations  0.64 us (2%)
    pallas_call x1, Pallas kernels, local(): pl.pallas_call(functools.partial(kernel, counts, phase_fields, regions, s...  34.5 us
    pallas_call x1, Pallas kernels, local(): pl.pallas_call(hand_out, out_shape=(jax.ShapeDtypeStruct(shape, f32), jax...  5.61 us

profile of v2, /device:TPU:0, one launch (start us, length us, event | category | flops | bytes accessed | tf_op | source)
XLA Modules:
  0.0 40.7 jit_solution(17491067337185597757)
XLA Ops:
  0.6 34.5 %adjoint_window.1 = (f32[8,16,128]{2,1,0:T(8,128)}, f32[8,16,128]{2,1,0:T(8,128)}, f32[8,128]{1,0:T(8,128)}) custom-call(s32[8,16,128]{2,1,0:T(8,128)} %refs_0_.1, s32[8,16,128]{2,1,0:T(8,128)} %refs_1_.1, f32[16]{0:T(128)} %refs_2_.1, s32[8,16,128]{2,1,0:T(8,128)} %refs_3_.1, f32[8,16,128]{2,1,0:T(8,128)} %refs_4_.1, f32[12,9]{1,0:T(8,128)} %refs_5_.1, ...), custom_call_target="tpu_custom_call" | custom-call | tf_op jit(solution)/shard_map/adjoint_window/pallas_call | solution.py:549
  35.1 5.6 %hand_out.1 = (f32[8,16,128]{2,1,0:T(8,128)}, f32[8,16,128]{2,1,0:T(8,128)}, f32[16]{0:T(128)}) custom-call(f32[8,16,128]{2,1,0:T(8,128)} %get-tuple-element.6.in_v, f32[8,16,128]{2,1,0:T(8,128)} %get-tuple-element.7.in_h, f32[8,128]{1,0:T(8,128)} %get-tuple-element.8.in_s), custom_call_target="tpu_custom_call" | custom-call | tf_op jit(solution)/shard_map/hand_out/pallas_call | solution.py:564

commit v3 on v2

--- a/solution.py
+++ b/solution.py
@@ -81,7 +81,7 @@
     for load in loads:
         load.start()
     (region_ref, tissue_ref, cond_ref, sector_ref, v_ref, table_ref, h_ref, av_ref, ah_ref, rec_ref) = held
-    (final_v, final_h, final_s, save_sem, *refs) = refs
+    (final_v, final_h, save_sem, *refs) = refs
     (coef, grad, diag, vvar, mvar, gathered, red_send, red_recv, *rest) = refs
     nx, ny, nz = counts
     shape = v_ref.shape
@@ -262,7 +262,10 @@
             yz=fetch(phase, f, 0, True, True),
         )
 
-    def extend(u, parts):
+    def lane_shifts(u):
+        return {dz: [roll(u[p], -dz, 1) for p in range(lx)] for dz in (1, -1)}
+
+    def extend(u, parts, shifts=None):
         middle = jnp.concatenate([u, parts["y"]], axis=1)
         ends = {m: jnp.concatenate([parts["x"][m], parts["xy"][m]], axis=0) for m in (1, -1)}
         planes = [ends[1]] + [middle[p] for p in range(lx)] + [ends[-1]]
@@ -272,10 +275,10 @@
             + [roll(z_rows, -(2 * p + 1), 1) for p in range(lx)]
             + [roll(parts["xz"][-1], -1, 1)]
         )
-        return planes, edges
+        return planes, edges, shifts
 
     def variant(ext, dy, dz, p):
-        planes, edges = ext
+        planes, edges, shifts = ext
         x = planes[p]
         outer = p in (0, lx + 1)
         if outer and dy and dz:
@@ -283,9 +286,13 @@
         if dz:
             rows = ly if dy == 0 else ly + 8
             at = lax.broadcasted_iota(jnp.int32, (rows, lz), 1)
-            x = jnp.where(
-                at == (lz - 1 if dz == 1 else 0), edges[p][:rows], roll(x[:rows], -dz, 1)
-            )
+            if shifts is None or outer:
+                along_lanes = roll(x[:rows], -dz, 1)
+            else:
+                along_lanes = shifts[dz][p - 1]
+                if dy:
+                    along_lanes = jnp.concatenate([along_lanes, roll(x[ly:], -dz, 1)], axis=0)
+            x = jnp.where(at == (lz - 1 if dz == 1 else 0), edges[p][:rows], along_lanes)
         if dy:
             x = roll(x, -dy, 0)
         return x[:ly]
@@ -348,10 +355,16 @@
     volts, gate = v_ref[...], h_ref[...]
     drive_v, drive_h = ionic(volts, gate)
 
+    shifts = lane_shifts(volts)
+    fac_shifts = lane_shifts(factor)
+    flux_shifts = [
+        lane_shifts(f) if base[2] else None for f, base in zip(flux, PAIR_OFFSETS)
+    ]
+
     receive(0)
     fac_halo = halo(0, 0)
     sec_halo = halo(0, 1)
-    fac_ext = extend(factor, fac_halo)
+    fac_ext = extend(factor, fac_halo, fac_shifts)
 
     halo_flux = [dict() for _ in PAIR_OFFSETS]
     for name in fac_halo:
@@ -374,13 +387,18 @@
         ]
     for o, (d, offset) in enumerate(OFFSETS):
         dx, dy, dz = offset
-        ext = extend(flux[d], halo_flux[d])
+        ext = extend(flux[d], halo_flux[d], flux_shifts[d])
         for p in range(lx):
             near = beside[dy, dz][p + 1 + dx]
             c = 0.5 * (flux[d][p] * near + variant(ext, dy, dz, p + 1 + dx) * tissue[p])
             coef[o, p] = c
             diag[p] = c if o == 0 else diag[p] + c
-            grad[o, p] = (-0.5 * tissue[p]) * near * fibre[d][p]
+
+    def store_grad():
+        for o, (d, (dx, dy, dz)) in enumerate(OFFSETS):
+            for p in range(lx):
+                near = beside[dy, dz][p + 1 + dx]
+                grad[o, p] = (-0.5 * tissue[p]) * near * fibre[d][p]
 
     volts_at, gate_at = [], []
     for step in range(WINDOW_STEPS):
@@ -389,12 +407,15 @@
         if step:
             stage_fields(step, (volts,))
             send(step)
+            if step == 1:
+                store_grad()
             drive_v, drive_h = ionic(volts, gate)
         base = volts + tissue * (step_size * drive_v)
         gate = gate + tissue * (step_size * drive_h)
         if step:
+            shifts = lane_shifts(volts)
             receive(step)
-        store_variants(vvar, step, extend(volts, halo(step, 0 if step else 2)))
+        store_variants(vvar, step, extend(volts, halo(step, 0 if step else 2), shifts))
         volts = jnp.stack(
             [base[p] + tissue[p] * spread(vvar, step, volts[p], p) for p in range(lx)]
         )
@@ -427,8 +448,9 @@
         vv, vh, hv, hh = partials(volts_at[step], gate_at[step])
         base = back_v + step_size * tissue * (vv * back_v + hv * back_h)
         back_h = back_h + step_size * tissue * (vh * back_v + hh * back_h)
+        shifts = lane_shifts(masked)
         receive(phase)
-        store_variants(mvar, step, extend(masked, halo(phase, 0)))
+        store_variants(mvar, step, extend(masked, halo(phase, 0), shifts))
         if step:
             back_v = jnp.stack(
                 [base[p] + spread(mvar, step, masked[p], p) for p in range(lx)]
@@ -472,7 +494,7 @@
     final_h[...] = back_h
     saves = [
         pltpu.make_async_copy(src, dst, save_sem.at[k])
-        for k, (src, dst) in enumerate(((final_v, out_v), (final_h, out_h), (final_s, out_s)))
+        for k, (src, dst) in enumerate(((final_v, out_v), (final_h, out_h)))
     ]
     saves[0].start()
     saves[1].start()
@@ -480,24 +502,10 @@
         finish_sends(k)
     each_other(red_wait)
     total = jnp.sum(gathered[...], axis=0)[0:1] * scale
-    final_s[...] = jnp.broadcast_to(total, (8, lz))
-    saves[2].start()
+    out_s[...] = total[0, :regions]
     each_other(red_finish)
     for save in saves:
         save.wait()
-
-
-def hand_out(in_v, in_h, in_s, out_v, out_h, out_s, row, sem):
-    copies = [
-        pltpu.make_async_copy(src, dst, sem.at[k])
-        for k, (src, dst) in enumerate(((in_s, row), (in_v, out_v), (in_h, out_h)))
-    ]
-    for copy in copies:
-        copy.start()
-    copies[0].wait()
-    out_s[...] = row[0, : out_s.shape[0]]
-    for copy in copies[1:]:
-        copy.wait()
 
 
 def local(*args):
@@ -523,8 +531,7 @@
         pltpu.SemaphoreType.DMA((len(order),)),
         pltpu.VMEM(shape, f32),
         pltpu.VMEM(shape, f32),
-        pltpu.VMEM((8, lz), f32),
-        pltpu.SemaphoreType.DMA((3,)),
+        pltpu.SemaphoreType.DMA((2,)),
         pltpu.VMEM((pairs,) + shape, f32),
         pltpu.VMEM((pairs,) + shape, f32),
         pltpu.VMEM(shape, f32),
@@ -546,34 +553,21 @@
         scratch += [pltpu.SemaphoreType.DMA((len(moved),))] * 2
     vmem = pl.BlockSpec(memory_space=pltpu.VMEM)
     hbm = pl.BlockSpec(memory_space=pltpu.HBM)
-    back_v, back_h, totals = pl.pallas_call(
+    return pl.pallas_call(
         functools.partial(kernel, counts, phase_fields, regions, sectors, scale),
         out_shape=(
             jax.ShapeDtypeStruct(shape, f32),
             jax.ShapeDtypeStruct(shape, f32),
-            jax.ShapeDtypeStruct((8, lz), f32),
+            jax.ShapeDtypeStruct((regions,), f32),
         ),
         in_specs=[hbm] * len(order),
-        out_specs=(hbm, hbm, hbm),
+        out_specs=(hbm, hbm, vmem),
         scratch_shapes=scratch,
         compiler_params=pltpu.CompilerParams(
             collective_id=0, has_side_effects=True, vmem_limit_bytes=63 * 2**20
         ),
         name="adjoint_window",
     )(*operands)
-    return pl.pallas_call(
-        hand_out,
-        out_shape=(
-            jax.ShapeDtypeStruct(shape, f32),
-            jax.ShapeDtypeStruct(shape, f32),
-            jax.ShapeDtypeStruct((regions,), f32),
-        ),
-        in_specs=[hbm] * 3,
-        out_specs=(hbm, hbm, vmem),
-        scratch_shapes=[pltpu.VMEM((8, lz), f32), pltpu.SemaphoreType.DMA((3,))],
-        compiler_params=pltpu.CompilerParams(vmem_limit_bytes=63 * 2**20),
-        name="hand_out",
-    )(back_v, back_h, totals)
 
 
 def solution(mesh):

time: 40.9 us -> 37.8 us (0.924)
  Pallas kernels: 40.1 us -> 34.3 us
  local copies, waits for them, and re-layouts: 0 us -> 2.65 us
    pallas_call x1 -> x0, Pallas kernels: 5.61 us -> none  [local(): pl.pallas_call(hand_out, out_shape=(jax.ShapeDtypeStruct(shape, f32), jax...]
    unnamed x0 -> x7, local copies, waits for them, and re-layouts: none -> 2.65 us
where the time goes in v3:
time: 37.8 us; the launch traced here: 37.6 us
  Pallas kernels  34.3 us (91%)
  local copies, waits for them, and re-layouts  2.65 us (7%)
  between operations  0.65 us (2%)
    pallas_call x1, Pallas kernels, local(): pl.pallas_call(functools.partial(kernel, counts, phase_fields, regions, s...  34.3 us
    unnamed x7, local copies, waits for them, and re-layouts  2.65 us

profile of v3, /device:TPU:0, one launch (start us, length us, event | category | flops | bytes accessed | tf_op | source)
XLA Modules:
  0.0 37.6 jit_solution(3281361864909449558)
XLA Ops:
  0.6 34.3 %adjoint_window.1 = (f32[8,16,128]{2,1,0:T(8,128)}, f32[8,16,128]{2,1,0:T(8,128)}, f32[16]{0:T(128)}) custom-call(s32[8,16,128]{2,1,0:T(8,128)} %refs_0_.1, s32[8,16,128]{2,1,0:T(8,128)} %refs_1_.1, f32[16]{0:T(128)} %refs_2_.1, s32[8,16,128]{2,1,0:T(8,128)} %refs_3_.1, f32[8,16,128]{2,1,0:T(8,128)} %refs_4_.1, f32[12,9]{1,0:T(8,128)} %refs_5_.1, ...), custom_call_target="tpu_custom_call" | custom-call | tf_op jit(solution)/shard_map/adjoint_window/pallas_call | solution.py:556
  34.9 0.0 copy-start
  35.0 1.5 %copy.16 = f32[8,16,128]{2,1,0:T(8,128)} copy(f32[8,16,128]{2,1,0:T(8,128)} %get-tuple-element.6) | data formatting | bytes 131072
  36.5 0.0 copy-done
  36.5 0.0 copy-start.1
  36.5 0.6 %copy.17 = f32[8,16,128]{2,1,0:T(8,128)} copy(f32[8,16,128]{2,1,0:T(8,128)S(1)} %copy-done) | data formatting | bytes 131072
  37.1 0.0 copy-done.1
  37.1 0.5 %copy.18 = f32[16]{0:T(128)} copy(f32[16]{0:T(128)S(1)} %copy-done.1) | data formatting | bytes 128
Async XLA Ops:
  34.9 1.5 %copy-start = (f32[8,16,128]{2,1,0:T(8,128)S(1)}, f32[8,16,128]{2,1,0:T(8,128)}, u32[]{:S(2)}) copy-start(f32[8,16,128]{2,1,0:T(8,128)} %get-tuple-element.7) | copy-start | bytes 196612
  36.5 0.6 %copy-start.1 = (f32[16]{0:T(128)S(1)}, f32[16]{0:T(128)}, u32[]{:S(2)}) copy-start(f32[16]{0:T(128)} %get-tuple-element.8) | copy-start | bytes 196
